TPU v7x, 1024 devices: a whole 8x8x8 slice. The times are simulated.
1024 devices in a mesh: dp: 32 (over x, z_lo, core), expert: 32 (over y, z_hi).
Axes of the slice: x: 8, y: 8, z: 8 (z_hi: 4, z_lo: 2; z = z_hi * 2 + z_lo), core: 2. Of those that a mesh axis runs over, the one named last changes fastest.
Arguments:
- tokens: bfloat16 [1024, 256, 768], P(('dp', 'expert')), may hold values from -16 to 16
- cotangent: bfloat16 [1024, 256, 768], P(('dp', 'expert')), may hold values from -6 to 6
- router: bfloat16 [768, 32], replicated, may hold values from -1 to 1
- in_weights: bfloat16 [32, 768, 2560], P('expert'), may hold values from -0.21875 to 0.21875
- out_weights: bfloat16 [32, 2560, 768], P('expert'), may hold values from -0.125 to 0.125
Outputs:
- token_grad: bfloat16 [1024, 256, 768], P(('dp', 'expert'))
- router_grad: float32 [768, 32], replicated
- in_weight_grad: bfloat16 [2560, 32, 768], P('dp', 'expert')
- out_weight_grad: bfloat16 [2560, 32, 768], P('dp', 'expert')
All inputs are finite; a program needn't handle non-finite values.
Results may differ from a plain program's by a relative error of at most 0.014.
Values may be sent and summed in bfloat16 or wider, within the bound.
A program may use at most 64 MiB of HBM per device.

v0:
```python
import jax
import jax.numpy as jnp
from jax import lax
from jax.sharding import PartitionSpec as P

half_root = 0.7071067811865476
inv_root_two_pi = 0.3989422804014327


def gelu_parts(pre_act):
    normal_cdf = 0.5 * (1.0 + jax.scipy.special.erf(pre_act * half_root))
    normal_pdf = jnp.exp(-0.5 * pre_act * pre_act) * inv_root_two_pi
    return (normal_cdf, normal_pdf)


def on_device(tokens, cotangent, router, in_weights, out_weights):
    logits = jnp.einsum("bpd,ds->bsp", tokens, router, preferred_element_type=jnp.float32)
    dispatch = jax.nn.softmax(logits, axis=2)
    combine = jax.nn.softmax(logits, axis=1)
    dispatch_low = dispatch.astype(jnp.bfloat16)
    combine_low = combine.astype(jnp.bfloat16)
    slot_inputs = jnp.einsum(
        "bsp,bpd->bsd", dispatch_low, tokens, preferred_element_type=jnp.float32
    ).astype(jnp.bfloat16)
    slot_cotan = jnp.einsum(
        "bsp,bpd->bsd", combine_low, cotangent, preferred_element_type=jnp.float32
    ).astype(jnp.bfloat16)
    owner_inputs, owner_cotan = (
        lax.all_to_all(slot_inputs, "expert", split_axis=1, concat_axis=0, tiled=True),
        lax.all_to_all(slot_cotan, "expert", split_axis=1, concat_axis=0, tiled=True),
    )
    pre_act = jnp.einsum(
        "rkd,kdf->rkf", owner_inputs, in_weights, preferred_element_type=jnp.float32
    )
    normal_cdf, normal_pdf = gelu_parts(pre_act)
    hidden = (pre_act * normal_cdf).astype(jnp.bfloat16)
    slot_outputs = jnp.einsum(
        "rkf,kfd->rkd", hidden, out_weights, preferred_element_type=jnp.float32
    ).astype(jnp.bfloat16)
    hidden_grad = jnp.einsum(
        "rkd,kfd->rkf", owner_cotan, out_weights, preferred_element_type=jnp.float32
    )
    pre_grad = (hidden_grad * (normal_cdf + pre_act * normal_pdf)).astype(jnp.bfloat16)
    input_grads = jnp.einsum(
        "rkf,kdf->rkd", pre_grad, in_weights, preferred_element_type=jnp.float32
    ).astype(jnp.bfloat16)
    returned_out, returned_grad = (
        lax.all_to_all(slot_outputs, "expert", split_axis=0, concat_axis=1, tiled=True),
        lax.all_to_all(input_grads, "expert", split_axis=0, concat_axis=1, tiled=True),
    )
    local_experts = in_weights.shape[0]
    share = in_weights.shape[2] // lax.axis_size("dp")
    groups = lax.axis_size("dp")
    row_total = owner_inputs.shape[0]
    width = owner_inputs.shape[2]
    all_inputs, all_cotan = (
        lax.all_gather(owner_inputs, "dp", axis=0, tiled=True),
        lax.all_gather(owner_cotan, "dp", axis=0, tiled=True),
    )
    part_grad, part_hidden = (
        lax.all_to_all(pre_grad, "dp", split_axis=2, concat_axis=0, tiled=True),
        lax.all_to_all(hidden, "dp", split_axis=2, concat_axis=0, tiled=True),
    )
    all_inputs = all_inputs.reshape(groups, row_total, local_experts, width)
    all_cotan = all_cotan.reshape(groups, row_total, local_experts, width)
    part_grad = part_grad.reshape(groups, row_total, local_experts, share)
    part_hidden = part_hidden.reshape(groups, row_total, local_experts, share)
    first_part = jnp.einsum(
        "prkf,prkd->pfkd", part_grad, all_inputs, preferred_element_type=jnp.float32
    )
    first_part = lax.optimization_barrier(first_part.astype(jnp.bfloat16))
    in_weight_grad = jnp.sum(first_part, axis=0, dtype=jnp.float32).astype(jnp.bfloat16)
    second_part = jnp.einsum(
        "prkf,prkd->pfkd", part_hidden, all_cotan, preferred_element_type=jnp.float32
    )
    second_part = lax.optimization_barrier(second_part.astype(jnp.bfloat16))
    out_weight_grad = jnp.sum(second_part, axis=0, dtype=jnp.float32).astype(jnp.bfloat16)
    combine_grad = jnp.einsum(
        "bpd,bsd->bsp", cotangent, returned_out, preferred_element_type=jnp.float32
    )
    dispatch_grad = jnp.einsum(
        "bpd,bsd->bsp", tokens, returned_grad, preferred_element_type=jnp.float32
    )
    logit_grad = combine * (combine_grad - jnp.sum(combine * combine_grad, axis=1, keepdims=True))
    logit_grad = logit_grad + dispatch * (
        dispatch_grad - jnp.sum(dispatch * dispatch_grad, axis=2, keepdims=True)
    )
    logit_low = logit_grad.astype(jnp.bfloat16)
    token_grad = jnp.einsum(
        "bsp,bsd->bpd", dispatch_low, returned_grad, preferred_element_type=jnp.float32
    )
    token_grad = token_grad + jnp.einsum(
        "bsp,ds->bpd", logit_low, router, preferred_element_type=jnp.float32
    )
    router_part = jnp.einsum("bpd,bsp->ds", tokens, logit_low, preferred_element_type=jnp.float32)
    router_grad = lax.psum(router_part, ("dp", "expert"))
    return (token_grad.astype(jnp.bfloat16), router_grad, in_weight_grad, out_weight_grad)


def solution(mesh):
    in_specs = (
        P(("dp", "expert"), None, None),
        P(("dp", "expert"), None, None),
        P(),
        P("expert", None, None),
        P("expert", None, None),
    )
    out_specs = (
        P(("dp", "expert"), None, None),
        P(),
        P("dp", "expert", None),
        P("dp", "expert", None),
    )
    return jax.shard_map(
        on_device, mesh=mesh, in_specs=in_specs, out_specs=out_specs, check_vma=False
    )
```

profile of v0, /device:TPU:1, one launch (start us, length us, event | category | flops | bytes accessed | tf_op | source)
XLA Modules:
  0.0 432.5 jit_solution(230575923593861733)
XLA Ops:
  8.0 0.0 copy-start
  8.0 0.0 all-gather.5.cloned.1.call-start
  8.1 0.9 copy-done
  9.0 1.2 fusion.74
  10.2 0.2 fusion.65
  10.4 0.2 fusion.35
  10.6 0.1 copy.57
  10.7 0.6 broadcast.18
  11.3 0.9 reduce.16
  12.3 33.4 %all_to_all.72 = bf16[32,2,384]{2,1,0:T(2,128)(2,1)S(1)} all-to-all(bf16[32,2,384]{2,1,0:T(2,128)(2,1)S(1)} %reshape.180), channel_id=1, replica_groups=mesh['dp'=32,'expert'=32] {'expert'}, dimensions={0} | all-to-all | bytes 98304 | tf_op jit(solution)/shard_map/all_to_all | solution.py:29
  45.7 0.6 copy.30
  46.3 0.0 all-gather.5.cloned.1.call-update
  46.3 0.0 all-gather.7.cloned.1.call-start
  46.4 1.2 fusion.34
  47.5 0.1 copy.58
  47.6 0.9 reduce.17
  48.6 14.0 %all_to_all.73 = bf16[32,2,384]{2,1,0:T(2,128)(2,1)S(1)} all-to-all(bf16[32,2,384]{2,1,0:T(2,128)(2,1)S(1)} %reshape.182), channel_id=1, replica_groups=mesh['dp'=32,'expert'=32] {'expert'}, dimensions={0} | all-to-all | bytes 98304 | tf_op jit(solution)/shard_map/all_to_all | solution.py:30
  62.7 0.6 copy.29
  63.3 0.0 all-gather.7.cloned.1.call-update
  63.4 0.0 copy-start.1
  63.4 3.1 multiply_convert_fusion
  66.5 3.4 fusion.17
  69.9 1.2 fusion.28
  71.1 0.7 reduce.18
  71.8 0.6 reshape.184
  72.5 3.9 all-to-all-start.2
  76.3 2.9 fusion.31
  79.2 0.7 reduce.19
  79.9 0.6 reshape.186
  80.6 6.8 %all-to-all-done.2 = bf16[32,2,384]{2,1,0:T(2,128)(2,1)S(1)} async-done(((bf16[32,2,384]{2,1,0:T(2,128)(2,1)}), bf16[32,2,384]{2,1,0:T(2,128)(2,1)S(1)}, u32[]{:S(2)}, u32[]{:S(2)}) %all-to-all-start.2) | async-done | bytes 49184 | tf_op jit(solution)/shard_map/all_to_all | solution.py:49
  87.4 5.0 %all-to-all-start.3 = ((bf16[32,2,384]{2,1,0:T(2,128)(2,1)}), bf16[32,2,384]{2,1,0:T(2,128)(2,1)S(1)}, u32[]{:S(2)}, u32[]{:S(2)}) async-start(bf16[32,2,384]{2,1,0:T(2,128)(2,1)} %reshape.186), calls=%async_computation.3 | async-start | bytes 98304 | tf_op jit(solution)/shard_map/all_to_all | solution.py:48
  92.4 0.9 copy.22
  93.3 0.9 copy.26
  94.3 0.0 copy-start.3
  94.3 15.2 %reduce.20 = bf16[2560,32]{1,0:T(8,128)(2,1)} reduce(bf16[2560,1,32]{2,1,0:T(2,128)(2,1)S(1)} %bitcast.149, bf16[]{:T(256)} %broadcast.18), dimensions={1}, to_apply=%bitcast.126.reduce_sub_computation | reduce | bytes 327682
  109.5 2.3 reshape.188
  111.8 14.3 %reduce.21 = bf16[2560,32]{1,0:T(8,128)(2,1)S(1)} reduce(bf16[2560,1,32]{2,1,0:T(2,128)(2,1)S(1)} %bitcast.148, bf16[]{:T(256)} %broadcast.18), dimensions={1}, to_apply=%bitcast.128.reduce_sub_computation | reduce | bytes 327682
  126.1 1.2 reshape.190
  127.3 0.0 all-to-all-done.3
  127.3 12.5 %all-to-all-start.4 = ((bf16[32,2,1280]{2,1,0:T(2,128)(2,1)}), bf16[32,2,1280]{2,1,0:T(2,128)(2,1)S(1)}, u32[]{:S(2)}, u32[]{:S(2)}) async-start(bf16[32,2,1280]{2,1,0:T(2,128)(2,1)} %reshape.188), calls=%async_computation.4 | async-start | bytes 327680 | tf_op jit(solution)/shard_map/all_to_all | solution.py:61
  139.8 0.0 all-reduce.2.cloned.1.call-start
  139.9 0.2 fusion.40
  140.1 0.3 multiply_reduce_fusion.1
  140.4 0.9 convolution_bitcast_fusion
  141.3 0.0 all-reduce.2.cloned.1.call-update
  141.3 8.6 %all-to-all-done.4 = bf16[32,2,1280]{2,1,0:T(2,128)(2,1)S(1)} async-done(((bf16[32,2,1280]{2,1,0:T(2,128)(2,1)}), bf16[32,2,1280]{2,1,0:T(2,128)(2,1)S(1)}, u32[]{:S(2)}, u32[]{:S(2)}) %all-to-all-start.4) | async-done | bytes 163872 | tf_op jit(solution)/shard_map/all_to_all | solution.py:61
  149.9 4.3 all-to-all-start.5
  154.2 0.4 fusion.58
  154.5 1.1 fusion.21
  155.7 0.8 reshape.189
  156.5 0.7 copy.23
  157.2 0.3 all_to_all.60
  157.5 7.3 %all-to-all-done.5 = bf16[32,2,1280]{2,1,0:T(2,128)(2,1)S(1)} async-done(((bf16[32,2,1280]{2,1,0:T(2,128)(2,1)}), bf16[32,2,1280]{2,1,0:T(2,128)(2,1)S(1)}, u32[]{:S(2)}, u32[]{:S(2)}) %all-to-all-start.5) | async-done | bytes 163872 | tf_op jit(solution)/shard_map/all_to_all | solution.py:62
  164.8 0.8 reshape.191
  165.6 0.7 copy.27
  166.3 0.3 all_to_all.64
  166.6 0.0 all-gather.5.cloned.1.call-done
  166.7 4.5 %convert_bitcast_fusion.1 = bf16[32,80,1,768]{3,1,0,2:T(8,128)(2,1)} fusion(bf16[32,32,768]{2,1,0:T(8,128)(2,1)} %bitcast.152, bf16[32,1,32,80]{3,2,0,1:T(8,128)(2,1)S(1)} %all_to_all.60), kind=kOutput, calls=%fused_computation.9 | convolution fusion | flops 127795200 | bytes 5668864 | tf_op jit(solution)/shard_map/prkf,prkd->pfkd/dot_general | solution.py:68
  171.2 14.4 %all-gather.7.cloned.1.call-done = bf16[1,1024,768]{2,1,0:T(8,128)(2,1)} async-done(((bf16[1,32,768]{2,1,0:T(8,128)(2,1)}), bf16[1,1024,768]{2,1,0:T(8,128)(2,1)}) %all-gather.7.cloned.1.call-update) | async-done | bytes 1572880 | tf_op jit(solution)/shard_map/all_gather | solution.py:58
  185.5 4.5 %convert_bitcast_fusion = bf16[32,80,1,768]{3,1,0,2:T(8,128)(2,1)} fusion(bf16[32,32,768]{2,1,0:T(8,128)(2,1)} %bitcast.153, bf16[32,1,32,80]{3,2,0,1:T(8,128)(2,1)S(1)} %all_to_all.64), kind=kOutput, calls=%fused_computation.8 | convolution fusion | flops 127795200 | bytes 5668864 | tf_op jit(solution)/shard_map/prkf,prkd->pfkd/dot_general | solution.py:73
  190.1 3.4 reduce_sum.68
  193.5 3.4 reduce_sum.70
  196.8 226.6 %all-reduce.2.cloned.1.call-done = f32[768,32]{0,1:T(8,128)} async-done(((f32[768,32]{0,1:T(8,128)}), f32[768,32]{0,1:T(8,128)}) %all-reduce.2.cloned.1.call-update) | async-done | bytes 98320 | tf_op jit(solution)/shard_map/psum | solution.py:96
  423.5 1.5 copy.62
  (12 shorter events, 0.2 us)
Async XLA Ops:
  8.0 1.0 copy-start
  8.0 158.7 %all-gather.5.cloned.1.call-start = ((), (), s32[]{:S(2)}) async-start(), calls=%async_computation.7 | async-start | bytes 1622016 | tf_op jit(solution)/shard_map/all_gather | solution.py:57
  46.3 139.2 %all-gather.7.cloned.1.call-start = ((), (), s32[]{:S(2)}) async-start(), calls=%async_computation.8 | async-start | bytes 1622016 | tf_op jit(solution)/shard_map/all_gather | solution.py:58
  63.3 3.2 copy-start.2
  63.4 6.5 %copy-start.1 = (bf16[1,768,2560]{2,1,0:T(8,128)(2,1)S(1)}, bf16[1,768,2560]{2,1,0:T(8,128)(2,1)}, u32[]{:S(2)}) copy-start(bf16[1,768,2560]{2,1,0:T(8,128)(2,1)} %param.8) | copy-start | bytes 11796484
  72.5 14.9 %all-to-all-start.2 = ((bf16[32,2,384]{2,1,0:T(2,128)(2,1)}), bf16[32,2,384]{2,1,0:T(2,128)(2,1)S(1)}, u32[]{:S(2)}, u32[]{:S(2)}) async-start(bf16[32,2,384]{2,1,0:T(2,128)(2,1)} %reshape.184), calls=%async_computation.2 | async-start | bytes 98304 | tf_op jit(solution)/shard_map/all_to_all | solution.py:49
  87.4 39.9 %all-to-all-start.3 = ((bf16[32,2,384]{2,1,0:T(2,128)(2,1)}), bf16[32,2,384]{2,1,0:T(2,128)(2,1)S(1)}, u32[]{:S(2)}, u32[]{:S(2)}) async-start(bf16[32,2,384]{2,1,0:T(2,128)(2,1)} %reshape.186), calls=%async_computation.3 | async-start | bytes 98304 | tf_op jit(solution)/shard_map/all_to_all | solution.py:48
  94.3 45.8 %copy-start.3 = (bf16[1,256,768]{2,1,0:T(8,128)(2,1)S(1)}, bf16[1,256,768]{2,1,0:T(8,128)(2,1)}, u32[]{:S(2)}) copy-start(bf16[1,256,768]{2,1,0:T(8,128)(2,1)} %param.6) | copy-start | bytes 1179652
  109.5 45.0 %copy-start.4 = (bf16[768,32]{0,1:T(8,128)(2,1)S(1)}, bf16[768,32]{0,1:T(8,128)(2,1)}, u32[]{:S(2)}) copy-start(bf16[768,32]{0,1:T(8,128)(2,1)} %param.7) | copy-start | bytes 147460
  127.3 22.6 %all-to-all-start.4 = ((bf16[32,2,1280]{2,1,0:T(2,128)(2,1)}), bf16[32,2,1280]{2,1,0:T(2,128)(2,1)S(1)}, u32[]{:S(2)}, u32[]{:S(2)}) async-start(bf16[32,2,1280]{2,1,0:T(2,128)(2,1)} %reshape.188), calls=%async_computation.4 | async-start | bytes 327680 | tf_op jit(solution)/shard_map/all_to_all | solution.py:61
  139.8 283.7 %all-reduce.2.cloned.1.call-start = ((), (), s32[]{:S(2)}) async-start(), calls=%async_computation.6 | async-start | bytes 196608 | tf_op jit(solution)/shard_map/psum | solution.py:96
  149.9 14.9 %all-to-all-start.5 = ((bf16[32,2,1280]{2,1,0:T(2,128)(2,1)}), bf16[32,2,1280]{2,1,0:T(2,128)(2,1)S(1)}, u32[]{:S(2)}, u32[]{:S(2)}) async-start(bf16[32,2,1280]{2,1,0:T(2,128)(2,1)} %reshape.190), calls=%async_computation.5 | async-start | bytes 327680 | tf_op jit(solution)/shard_map/all_to_all | solution.py:62
Sparse Core Ops, SparseCore 0:
  46.4 64.6 all-gather.4
  114.8 70.7 all-gather.6
Sparse Core Ops, SparseCore 1:
  145.6 277.9 all-reduce.1
where the time goes:
time: 433 us; the launch traced here: 432 us
  waiting for transfers between devices  264 us (61%)
  blocking collectives  47.4 us (11%)
  other arithmetic  39.8 us (9%)
  starting transfers between devices  25.7 us (6%)
  matrix products  25.1 us (6%)
  between operations  15.8 us (4%)
  local copies, waits for them, and re-layouts  14.9 us (3%)
    psum x1, waiting for transfers between devices, on_device(): router_grad = lax.psum(router_part, ('dp', 'expert'))  227 us
    all_to_all x1, blocking collectives, on_device(): lax.all_to_all(slot_inputs, 'expert', split_axis=1, concat_axis=0, tiled=...  33.4 us
    unnamed x4, other arithmetic  31.4 us
    all_gather x1, waiting for transfers between devices, on_device(): lax.all_gather(owner_cotan, 'dp', axis=0, tiled=True)  14.4 us
    all_to_all x1, blocking collectives, on_device(): lax.all_to_all(slot_cotan, 'expert', split_axis=1, concat_axis=0, tiled=T...  14 us
    all_to_all x1, starting transfers between devices, on_device(): lax.all_to_all(pre_grad, 'dp', split_axis=2, concat_axis=0, tiled=True)  12.5 us
    unnamed x26, local copies, waits for them, and re-layouts  10.8 us
  transfers between devices with their start and end apart: 7, of which 5 were waited for; matrix products, arithmetic and copies ran while one was open for 17% of the time, Pallas kernels for 0%

commit v1 on v0

v1 whole, which is shorter than its diff:
```python
import functools

import jax
import jax.numpy as jnp
from jax import lax
from jax.experimental import pallas as pl
from jax.experimental.pallas import tpu as pltpu
from jax.sharding import PartitionSpec as P

MESH = pl.DeviceIdType.MESH
LOW = jnp.bfloat16
F32 = jnp.float32
QUAD = 4
LANES = 128
ROWS = 16
half_root = 0.7071067811865476
inv_root_two_pi = 0.3989422804014327


def dot(a, b, dims):
    return lax.dot_general(a, b, (dims, ((), ())), preferred_element_type=F32)


NN = ((1,), (0,))
NT = ((1,), (1,))
TN = ((0,), (0,))


def pack(stage, dst, first, second):
    slots, width = first.shape
    parts = width // LANES
    for i, value in enumerate((first, second)):
        for j in range(parts):
            stage[pl.ds(i * parts + j, slots, stride=ROWS), :] = value[:, j * LANES : (j + 1) * LANES]
    dst[...] = stage[...].reshape(slots, ROWS, LANES).astype(LOW)


def unpack(stage, src, width):
    slots = src.shape[0]
    parts = width // LANES
    stage[...] = src[...].astype(F32).reshape(slots * ROWS, LANES)
    both = []
    for i in range(2):
        columns = [stage[pl.ds(i * parts + j, slots, stride=ROWS), :] for j in range(parts)]
        both.append(jnp.concatenate(columns, axis=1).astype(LOW))
    return both


def kernel(
    n_dp, n_e,
    tok_h, cot_h, rt_h, w1_h, w2_h,
    tg_h, rg_h, gw_h,
    tok, cot, rt, w1, w2, stage, stage_b,
    s1, r1, s2, r2, rows, msgs, part, total,
    tiles, tiles_in, sum_x, sum_q, tiles_out,
    core_out, core_in, pair_out, pair_in,
    tg, rg, gw,
    load, store, send, recv,
):
    dp, e = lax.axis_index("dp"), lax.axis_index("expert")
    n_x = n_dp // QUAD
    x, q = dp // QUAD, lax.rem(dp, QUAD)
    slots = n_e
    width = tok.shape[1]
    ff = w1.shape[1]
    share = ff // n_dp
    n_tiles = tiles.shape[0]
    tile_rows = tiles.shape[1]
    across = width // LANES

    loads = [
        pltpu.make_async_copy(src, dst, load.at[i])
        for i, (src, dst) in enumerate(((rt_h, rt), (tok_h, tok), (cot_h, cot), (w1_h, w1), (w2_h, w2)))
    ]
    for copy in loads:
        copy.start()
    stage[...] = jnp.zeros_like(stage)

    barrier = pltpu.get_barrier_semaphore()

    def greet(device):
        pl.semaphore_signal(barrier, inc=1, device_id=device, device_id_type=MESH)

    @pl.loop(1, n_e)
    def _(o):
        greet((dp, lax.rem(e + o, n_e)))

    @pl.loop(1, n_x)
    def _(o):
        greet((lax.rem(x + o, n_x) * QUAD + q, e))

    for o in range(1, QUAD):
        greet((x * QUAD + lax.rem(q + o, QUAD), e))

    def remote(src, dst, at, device):
        return pltpu.make_async_remote_copy(
            src_ref=src, dst_ref=dst, send_sem=send.at[at], recv_sem=recv.at[at],
            device_id=device, device_id_type=MESH,
        )

    next_e = (dp, lax.rem(e + 1, n_e))
    next_x = (lax.rem(x + 1, n_x) * QUAD + q, e)
    next_q = (x * QUAD + lax.rem(q + 1, QUAD), e)

    def all_of(ref, count, at, device):
        return remote(ref.at[pl.ds(0, count)], ref.at[pl.ds(0, count)], at, device)

    loads[0].wait()
    loads[1].wait()
    logits = dot(rt[...], tok[...], NT)
    over_patches = jnp.exp(logits - jnp.max(logits, axis=1, keepdims=True))
    dispatch = over_patches / jnp.sum(over_patches, axis=1, keepdims=True)
    over_slots = jnp.exp(logits - jnp.max(logits, axis=0, keepdims=True))
    combine = over_slots / jnp.sum(over_slots, axis=0, keepdims=True)
    dispatch_low = dispatch.astype(LOW)
    combine_low = combine.astype(LOW)
    slot_inputs = dot(dispatch_low, tok[...], NN)
    loads[2].wait()
    slot_cotan = dot(combine_low, cot[...], NN)
    pack(stage, s1, slot_inputs, slot_cotan)
    pl.semaphore_wait(barrier, n_e - 1 + n_x - 1 + QUAD - 1)

    @pl.loop(1, n_e)
    def _(o):
        peer = lax.rem(e + o, n_e)
        remote(s1.at[peer], r1.at[e], 0, (dp, peer)).start()

    r1[e] = s1[e]
    all_of(r1, n_e - 1, 0, next_e).wait_recv()

    rows_in, rows_cotan = unpack(stage_b, r1, width)
    rows[x, 0] = rows_in
    rows[x, 1] = rows_cotan

    @pl.loop(1, n_x)
    def _(o):
        peer = lax.rem(x + o, n_x)
        remote(rows.at[x], rows.at[x], 1, (peer * QUAD + q, e)).start()

    loads[3].wait()
    loads[4].wait()
    block = ff // n_x
    pair = 2 * block
    per = 2 if ff % (2 * pair) == 0 else 1
    step = per * pair
    outputs = jnp.zeros((slots, width), F32)
    grads = jnp.zeros((slots, width), F32)
    is_first = lax.broadcasted_iota(jnp.int32, (slots, pair), 1) < block
    for k in range(ff // step):
        first = w1[:, k * step : (k + 1) * step]
        second = w2[k * step : (k + 1) * step, :]
        pre_act = dot(rows_in, first, NN)
        hidden_grad = dot(rows_cotan, second, NT)
        normal_cdf = 0.5 * (1.0 + lax.erf(pre_act * half_root))
        normal_pdf = jnp.exp(-0.5 * pre_act * pre_act) * inv_root_two_pi
        hidden = pre_act * normal_cdf
        pre_grad = hidden_grad * (normal_cdf + pre_act * normal_pdf)
        outputs += dot(hidden.astype(LOW), second, NN)
        grads += dot(pre_grad.astype(LOW), first, NT)
        for i in range(per):
            p_part = pre_grad[:, i * pair : (i + 1) * pair]
            h_part = hidden[:, i * pair : (i + 1) * pair]
            at = 2 * (k * per + i)
            msgs[at] = jnp.where(is_first, p_part, pltpu.roll(h_part, block, 1)).astype(LOW)
            msgs[at + 1] = jnp.where(is_first, pltpu.roll(p_part, block, 1), h_part).astype(LOW)
    pack(stage, s2, outputs, grads)

    @pl.loop(1, n_e)
    def _(o):
        peer = lax.rem(e + o, n_e)
        remote(s2.at[peer], r2.at[e], 2, (dp, peer)).start()

    @pl.loop(1, n_x)
    def _(o):
        peer = lax.rem(x + o, n_x)
        remote(msgs.at[peer], part.at[x], 3, (peer * QUAD + q, e)).start()

    part[x] = msgs[x]
    r2[e] = s2[e]
    all_of(r2, n_e - 1, 2, next_e).wait_recv()

    slot_outputs, input_grads = unpack(stage_b, r2, width)
    combine_grad = dot(slot_outputs, cot[...], NT)
    dispatch_grad = dot(input_grads, tok[...], NT)
    logit_grad = combine * (combine_grad - jnp.sum(combine * combine_grad, axis=0, keepdims=True))
    logit_grad += dispatch * (dispatch_grad - jnp.sum(dispatch * dispatch_grad, axis=1, keepdims=True))
    logit_low = logit_grad.astype(LOW)
    router_part = dot(logit_low, tok[...], NN)
    for t in range(n_tiles):
        i, j = divmod(t, across)
        tiles[t] = router_part[i * tile_rows : (i + 1) * tile_rows, j * LANES : (j + 1) * LANES]

    @pl.loop(1, n_e)
    def _(o):
        peer = lax.rem(e + o, n_e)

        @pl.when(peer < n_tiles)
        def _():
            remote(tiles.at[peer], tiles_in.at[e], 4, (dp, peer)).start()

    weights = jnp.concatenate([dispatch_low, logit_low], axis=0)
    values = jnp.concatenate([input_grads, rt[...]], axis=0)
    tg[...] = dot(weights, values, TN).astype(LOW)
    tg_copy = pltpu.make_async_copy(tg, tg_h, store.at[0])
    tg_copy.start()

    @pl.when(e < n_tiles)
    def _():
        tiles_in[e] = tiles[e]
        all_of(tiles_in, n_e - 1, 4, next_e).wait_recv()
        sum_x[x] = jnp.sum(tiles_in[...], axis=0)

        @pl.loop(1, n_x)
        def _(o):
            peer = lax.rem(x + o, n_x)
            remote(sum_x.at[x], sum_x.at[x], 5, (peer * QUAD + q, e)).start()

        all_of(sum_x, n_x - 1, 5, next_x).wait_recv()
        sum_q[q] = jnp.sum(sum_x[...], axis=0)
        for o in range(1, QUAD):
            remote(sum_q.at[q], sum_q.at[q], 6, (x * QUAD + lax.rem(q + o, QUAD), e)).start()
        all_of(sum_q, QUAD - 1, 6, next_q).wait_recv()
        tiles_out[e] = jnp.sum(sum_q[...], axis=0)

        @pl.loop(1, n_e)
        def _(o):
            peer = lax.rem(e + o, n_e)
            remote(tiles_out.at[e], tiles_out.at[e], 7, (dp, peer)).start()

    all_of(rows, n_x - 1, 1, next_x).wait_recv()
    all_of(part, n_x - 1, 3, next_x).wait_recv()
    left = part[...].reshape(n_x * slots, pair).T
    for i in range(2):
        total[i] = dot(left[i * block : (i + 1) * block], rows[:, i].reshape(n_x * slots, width), NN).reshape(QUAD, share, width)
    z, core = q // 2, lax.rem(q, 2)
    for i in range(2):
        for there in range(2):
            core_out[there, i] = total[i, there * 2 + 1 - core].astype(LOW)
    core_copy = remote(core_out, core_in, 8, (x * QUAD + z * 2 + 1 - core, e))
    core_copy.start()
    core_copy.wait_recv()
    for i in range(2):
        pair_out[i] = (total[i, (1 - z) * 2 + core] + core_in[1 - z, i].astype(F32)).astype(LOW)
    pair_copy = remote(pair_out, pair_in, 9, (x * QUAD + (1 - z) * 2 + core, e))
    pair_copy.start()

    @pl.when(e < n_tiles)
    def _():
        all_of(tiles_out, n_tiles - 1, 7, next_e).wait_recv()

    @pl.when(e >= n_tiles)
    def _():
        all_of(tiles_out, n_tiles, 7, next_e).wait_recv()

    for t in range(n_tiles):
        i, j = divmod(t, across)
        rg[i * tile_rows : (i + 1) * tile_rows, j * LANES : (j + 1) * LANES] = tiles_out[t]
    rg_copy = pltpu.make_async_copy(rg, rg_h, store.at[1])
    rg_copy.start()

    pair_copy.wait_recv()
    for i in range(2):
        gw[i] = (total[i, q] + core_in[z, i].astype(F32) + pair_in[i].astype(F32)).astype(LOW)
    gw_copy = pltpu.make_async_copy(gw, gw_h, store.at[2])
    gw_copy.start()

    all_of(s1, n_e - 1, 0, next_e).wait_send()
    all_of(rows, n_x - 1, 1, next_x).wait_send()
    all_of(s2, n_e - 1, 2, next_e).wait_send()
    all_of(msgs, n_x - 1, 3, next_x).wait_send()
    core_copy.wait_send()
    pair_copy.wait_send()

    @pl.when(e < n_tiles)
    def _():
        all_of(tiles, n_tiles - 1, 4, next_e).wait_send()
        all_of(sum_x, n_x - 1, 5, next_x).wait_send()
        all_of(sum_q, QUAD - 1, 6, next_q).wait_send()
        all_of(tiles_in, n_e - 1, 7, next_e).wait_send()

    @pl.when(e >= n_tiles)
    def _():
        all_of(tiles, n_tiles, 4, next_e).wait_send()

    tg_copy.wait()
    rg_copy.wait()
    gw_copy.wait()


def on_device(n_dp, n_e, tokens, cotangent, router, in_weights, out_weights):
    _, patches, width = tokens.shape
    ff = in_weights.shape[2]
    slots = router.shape[1]
    n_x = n_dp // QUAD
    share = ff // n_dp
    tile_rows = min(8, slots)
    n_tiles = slots // tile_rows * (width // LANES)
    vmem = pltpu.VMEM
    dma = pltpu.SemaphoreType.DMA
    token_grad, router_grad, weight_grads = pl.pallas_call(
        functools.partial(kernel, n_dp, n_e),
        out_shape=(
            jax.ShapeDtypeStruct((patches, width), LOW),
            jax.ShapeDtypeStruct((slots, width), F32),
            jax.ShapeDtypeStruct((2, share, width), LOW),
        ),
        in_specs=[pl.BlockSpec(memory_space=pl.ANY)] * 5,
        out_specs=[pl.BlockSpec(memory_space=pl.ANY)] * 3,
        scratch_shapes=[
            vmem((patches, width), LOW),
            vmem((patches, width), LOW),
            vmem((slots, width), LOW),
            vmem((width, ff), LOW),
            vmem((ff, width), LOW),
            vmem((slots * ROWS, LANES), F32),
            vmem((slots * ROWS, LANES), F32),
            *[vmem((slots, ROWS, LANES), LOW)] * 4,
            vmem((n_x, 2, slots, width), LOW),
            vmem((n_x, slots, 2 * ff // n_x), LOW),
            vmem((n_x, slots, 2 * ff // n_x), LOW),
            vmem((2, QUAD, share, width), F32),
            vmem((n_tiles, tile_rows, LANES), F32),
            vmem((n_e, tile_rows, LANES), F32),
            vmem((n_x, tile_rows, LANES), F32),
            vmem((QUAD, tile_rows, LANES), F32),
            vmem((n_tiles, tile_rows, LANES), F32),
            vmem((2, 2, share, width), LOW),
            vmem((2, 2, share, width), LOW),
            vmem((2, share, width), LOW),
            vmem((2, share, width), LOW),
            vmem((patches, width), LOW),
            vmem((slots, width), F32),
            vmem((2, share, width), LOW),
            dma((5,)),
            dma((3,)),
            dma((10,)),
            dma((10,)),
        ],
        compiler_params=pltpu.CompilerParams(
            collective_id=0, has_side_effects=True, vmem_limit_bytes=56 * 2**20
        ),
        cost_estimate=pl.CostEstimate(flops=10**9, bytes_accessed=10**7, transcendentals=10**5),
    )(tokens[0], cotangent[0], router.T, in_weights[0], out_weights[0])
    return (
        token_grad[None],
        router_grad.T,
        weight_grads[0][:, None],
        weight_grads[1][:, None],
    )


def solution(mesh):
    image = P(("dp", "expert"), None, None)
    expert = P("expert", None, None)
    grad = P("dp", "expert", None)
    return jax.shard_map(
        functools.partial(on_device, mesh.shape["dp"], mesh.shape["expert"]),
        mesh=mesh,
        in_specs=(image, image, P(), expert, expert),
        out_specs=(image, P(), grad, grad),
        check_vma=False,
    )
```

time: 433 us -> 79.1 us (0.18)
  waiting for transfers between devices: 264 us -> 0 us
  Pallas kernels: 0 us -> 73.3 us
  blocking collectives: 47.4 us -> 0 us
  other arithmetic: 39.8 us -> 0 us
  starting transfers between devices: 25.7 us -> 0 us
  matrix products: 25.1 us -> 0 us
  between operations: 15.8 us -> 0.64 us
  local copies, waits for them, and re-layouts: 14.9 us -> 4.97 us
    psum x1 -> x0, waiting for transfers between devices: 227 us -> none  [on_device(): router_grad = lax.psum(router_part, ('dp', 'expert'))]
    pallas_call x0 -> x1, Pallas kernels: none -> 73.3 us  [on_device(): pl.pallas_call(functools.partial(kernel, n_dp, n_e), out_shape=(jax.Shape...]
    all_to_all x2 -> x0, blocking collectives: 47.4 us -> none  [the longest x1 33.4 us: on_device(): lax.all_to_all(slot_inputs, 'expert', split_axis=1, concat_axis=0, tiled=...]
    unnamed x4 -> x0, other arithmetic: 31.4 us -> none
    all_to_all x4 -> x0, starting transfers between devices: 25.6 us -> none  [the longest x1 12.5 us: on_device(): lax.all_to_all(pre_grad, 'dp', split_axis=2, concat_axis=0, tiled=True)]
    dot_general x14 -> x0, matrix products: 25.1 us -> none  [the longest x1 4.53 us: on_device(): jnp.einsum('prkf,prkd->pfkd', part_hidden, all_cotan, preferred_element_t...]
    all_to_all x4 -> x0, waiting for transfers between devices: 22.7 us -> none  [the longest x1 8.58 us: on_device(): lax.all_to_all(pre_grad, 'dp', split_axis=2, concat_axis=0, tiled=True)]
    all_gather x2 -> x0, waiting for transfers between devices: 14.4 us -> none  [the longest x1 14.4 us: on_device(): lax.all_gather(owner_cotan, 'dp', axis=0, tiled=True)]
  transfers between devices with their start and end apart: 7 -> 0, of which waited for: 5 -> 0; matrix products, arithmetic and copies ran while one was open for 17% -> 0% of each run, Pallas kernels for 0% -> 0%
where the time goes in v1:
time: 79.1 us; the launch traced here: 78.9 us
  Pallas kernels  73.3 us (93%)
  local copies, waits for them, and re-layouts  4.97 us (6%)
    pallas_call x1, Pallas kernels, on_device(): pl.pallas_call(functools.partial(kernel, n_dp, n_e), out_shape=(jax.Shape...  73.3 us
    unnamed x2, local copies, waits for them, and re-layouts  3.3 us
    another operation x1, local copies, waits for them, and re-layouts, on_device(): weight_grads[1][:, None]  1.67 us

profile of v1, /device:TPU:1, one launch (start us, length us, event | category | flops | bytes accessed | tf_op | source)
XLA Modules:
  0.0 78.9 jit_solution(9896689057745401857)
XLA Ops:
  0.6 73.3 %shard_map.84 = (bf16[256,768]{1,0:T(8,128)(2,1)}, f32[32,768]{1,0:T(8,128)}, bf16[2,80,768]{2,1,0:T(8,128)(2,1)}) custom-call(bf16[256,768]{1,0:T(8,128)(2,1)} %bitcast.13, bf16[256,768]{1,0:T(8,128)(2,1)} %bitcast.14, bf16[32,768]{1,0:T(8,128)(2,1)} %bitcast.17, bf16[768,2560]{1,0:T(8,128)(2,1)} %bitcast.11, bf16[2560,768]{1,0:T(8,128)(2,1)} %bitcast.12), custom_call_target="tpu_custom_call" | custom-call | flops 1000000000 | bytes 10000000 | tf_op jit(solution)/shard_map/pallas_call | solution.py:300
  73.9 1.7 %slice_bitcast_fusion = (bf16[80,1,768]{2,0,1:T(8,128)(2,1)}, bf16[80,1,768]{2,0,1:T(8,128)(2,1)}) fusion(bf16[2,80,768]{2,1,0:T(8,128)(2,1)} %get-tuple-element.9), kind=kLoop, calls=%fused_computation | loop fusion | bytes 491520 | tf_op jit(solution)/shard_map/broadcast_in_dim;squeeze | solution.py:348
  75.6 1.8 %copy.11 = bf16[1,256,768]{2,1,0:T(8,128)(2,1)} copy(bf16[1,256,768]{2,1,0:T(8,128)(2,1)} %bitcast.15) | data formatting | bytes 786432
  77.4 1.5 %copy.12 = f32[768,32]{0,1:T(8,128)} copy(f32[768,32]{0,1:T(8,128)} %bitcast.16) | data formatting | bytes 196608

commit v2 on v1

v2 whole, which is shorter than its diff:
```python
import functools

import jax
import jax.numpy as jnp
from jax import lax
from jax.experimental import pallas as pl
from jax.experimental.pallas import tpu as pltpu
from jax.sharding import PartitionSpec as P

MESH = pl.DeviceIdType.MESH
LOW = jnp.bfloat16
F32 = jnp.float32
QUAD = 4
LANES = 128
ROWS = 16
half_root = 0.7071067811865476
inv_root_two_pi = 0.3989422804014327


def dot(a, b, dims):
    return lax.dot_general(a, b, (dims, ((), ())), preferred_element_type=F32)


NN = ((1,), (0,))
NT = ((1,), (1,))
TN = ((0,), (0,))


def pack(stage, dst, first, second):
    slots, width = first.shape
    parts = width // LANES
    for i, value in enumerate((first, second)):
        for j in range(parts):
            stage[pl.ds(i * parts + j, slots, stride=ROWS), :] = value[:, j * LANES : (j + 1) * LANES]
    dst[...] = stage[...].reshape(slots, ROWS, LANES).astype(LOW)


def unpack(stage, src, width):
    slots = src.shape[0]
    parts = width // LANES
    stage[...] = src[...].astype(F32).reshape(slots * ROWS, LANES)
    both = []
    for i in range(2):
        columns = [stage[pl.ds(i * parts + j, slots, stride=ROWS), :] for j in range(parts)]
        both.append(jnp.concatenate(columns, axis=1).astype(LOW))
    return both


def kernel(
    n_dp, n_e,
    tok_h, cot_h, rt_h, w1_h, w2_h,
    tg, rg, g1, g2,
    tok, cot, rt, w1, w2, stage, stage_b,
    s1, r1, s2, r2, rows, msgs, part, total,
    tiles, tiles_in, sum_e, tiles_out,
    core_out, core_in, pair_out, pair_in,
    load, send, recv, ring_send, ring_recv,
):
    dp, e = lax.axis_index("dp"), lax.axis_index("expert")
    n_x = n_dp // QUAD
    x, q = dp // QUAD, lax.rem(dp, QUAD)
    slots = n_e
    width = tok.shape[1]
    ff = w1.shape[1]
    share = ff // n_dp
    n_tiles = tiles.shape[0]
    tile_rows = tiles.shape[1]
    across = width // LANES

    loads = [
        pltpu.make_async_copy(src, dst, load.at[i])
        for i, (src, dst) in enumerate(((rt_h, rt), (tok_h, tok), (cot_h, cot), (w1_h, w1), (w2_h, w2)))
    ]
    for copy in loads:
        copy.start()
    stage[...] = jnp.zeros_like(stage)

    def each(count, body):
        far = max(1, count * 3 // 8)
        for o in (*range(far, count), *range(1, far)):
            body(o)

    def to_experts(body):
        each(n_e, lambda o: body(lax.rem(e + o, n_e)))

    def to_replicas(body):
        each(n_dp, lambda o: body(lax.rem(dp + o, n_dp)))

    barrier = pltpu.get_barrier_semaphore()

    def greet(device):
        pl.semaphore_signal(barrier, inc=1, device_id=device, device_id_type=MESH)

    to_experts(lambda peer: greet((dp, peer)))
    to_replicas(lambda peer: greet((peer, e)))

    def remote(src, dst, at, device):
        return pltpu.make_async_remote_copy(
            src_ref=src, dst_ref=dst, send_sem=send.at[at], recv_sem=recv.at[at],
            device_id=device, device_id_type=MESH,
        )

    next_e = (dp, lax.rem(e + 1, n_e))
    next_x = (lax.rem(x + 1, n_x) * QUAD + q, e)
    next_dp = (lax.rem(dp + 1, n_dp), e)

    half = n_x // 2
    right = next_x
    left = (lax.rem(x + n_x - 1, n_x) * QUAD + q, e)

    def ring(s, sender):
        a = lax.rem(x - (s - 1 + sender) + n_x, n_x)
        b = lax.rem(x + s - 1 + sender, n_x)
        blocks = (rows.at[a], rows.at[b]) if s < half else (rows.at[a, 0], rows.at[b, 1])
        return [
            pltpu.make_async_remote_copy(
                src_ref=block, dst_ref=block, send_sem=ring_send.at[s - 1, i], recv_sem=ring_recv.at[s - 1, i],
                device_id=device, device_id_type=MESH,
            )
            for i, (block, device) in enumerate(zip(blocks, (right, left)))
        ]

    def ring_start(s):
        for copy in ring(s, 0):
            copy.start()

    def ring_arrived(s):
        for copy in ring(s, 1):
            copy.wait_recv()

    def all_of(ref, count, at, device):
        return remote(ref.at[pl.ds(0, count)], ref.at[pl.ds(0, count)], at, device)

    loads[0].wait()
    loads[1].wait()
    logits = dot(rt[...], tok[...], NT)
    over_patches = jnp.exp(logits - jnp.max(logits, axis=1, keepdims=True))
    dispatch = over_patches / jnp.sum(over_patches, axis=1, keepdims=True)
    over_slots = jnp.exp(logits - jnp.max(logits, axis=0, keepdims=True))
    combine = over_slots / jnp.sum(over_slots, axis=0, keepdims=True)
    dispatch_low = dispatch.astype(LOW)
    combine_low = combine.astype(LOW)
    slot_inputs = dot(dispatch_low, tok[...], NN)
    loads[2].wait()
    slot_cotan = dot(combine_low, cot[...], NN)
    pack(stage, s1, slot_inputs, slot_cotan)
    pl.semaphore_wait(barrier, n_e - 1 + n_dp - 1)

    @to_experts
    def _(peer):
        remote(s1.at[peer], r1.at[e], 0, (dp, peer)).start()

    r1[e] = s1[e]
    all_of(r1, n_e - 1, 0, next_e).wait_recv()

    rows_in, rows_cotan = unpack(stage_b, r1, width)
    rows[x, 0] = rows_in
    rows[x, 1] = rows_cotan

    ring_start(1)

    loads[3].wait()
    loads[4].wait()
    block = ff // n_x
    pair = 2 * block
    per = 2 if ff % (2 * pair) == 0 else 1
    step = per * pair
    outputs = jnp.zeros((slots, width), F32)
    grads = jnp.zeros((slots, width), F32)
    is_first = lax.broadcasted_iota(jnp.int32, (slots, pair), 1) < block
    for k in range(ff // step):
        first = w1[:, k * step : (k + 1) * step]
        second = w2[k * step : (k + 1) * step, :]
        pre_act = dot(rows_in, first, NN)
        hidden_grad = dot(rows_cotan, second, NT)
        normal_cdf = 0.5 * (1.0 + lax.erf(pre_act * half_root))
        normal_pdf = jnp.exp(-0.5 * pre_act * pre_act) * inv_root_two_pi
        hidden = pre_act * normal_cdf
        pre_grad = hidden_grad * (normal_cdf + pre_act * normal_pdf)
        outputs += dot(hidden.astype(LOW), second, NN)
        grads += dot(pre_grad.astype(LOW), first, NT)
        for i in range(per):
            p_part = pre_grad[:, i * pair : (i + 1) * pair]
            h_part = hidden[:, i * pair : (i + 1) * pair]
            at = 2 * (k * per + i)
            msgs[at] = jnp.where(is_first, p_part, pltpu.roll(h_part, block, 1)).astype(LOW)
            msgs[at + 1] = jnp.where(is_first, pltpu.roll(p_part, block, 1), h_part).astype(LOW)
    pack(stage, s2, outputs, grads)

    @to_experts
    def _(peer):
        remote(s2.at[peer], r2.at[e], 2, (dp, peer)).start()

    @functools.partial(each, n_x)
    def _(o):
        peer = lax.rem(x + o, n_x)
        remote(msgs.at[peer], part.at[x], 3, (peer * QUAD + q, e)).start()

    part[x] = msgs[x]
    r2[e] = s2[e]
    for s in range(1, half):
        ring_arrived(s)
        ring_start(s + 1)
    all_of(r2, n_e - 1, 2, next_e).wait_recv()

    slot_outputs, input_grads = unpack(stage_b, r2, width)
    combine_grad = dot(slot_outputs, cot[...], NT)
    dispatch_grad = dot(input_grads, tok[...], NT)
    logit_grad = combine * (combine_grad - jnp.sum(combine * combine_grad, axis=0, keepdims=True))
    logit_grad += dispatch * (dispatch_grad - jnp.sum(dispatch * dispatch_grad, axis=1, keepdims=True))
    logit_low = logit_grad.astype(LOW)
    router_part = dot(logit_low, tok[...], NN)
    for t in range(n_tiles):
        i, j = divmod(t, across)
        tiles[t] = router_part[i * tile_rows : (i + 1) * tile_rows, j * LANES : (j + 1) * LANES]

    @to_replicas
    def _(peer):
        @pl.when(peer < n_tiles)
        def _():
            remote(tiles.at[peer], tiles_in.at[dp], 4, (peer, e)).start()

    weights = jnp.concatenate([dispatch_low, logit_low], axis=0)
    values = jnp.concatenate([input_grads, rt[...]], axis=0)
    tg[...] = dot(weights, values, TN).astype(LOW)

    ring_arrived(half)
    all_of(part, n_x - 1, 3, next_x).wait_recv()
    wide = part[...].reshape(n_x * slots, pair).T
    z, core = q // 2, lax.rem(q, 2)
    other_core = (x * QUAD + z * 2 + 1 - core, e)
    other_pair = (x * QUAD + (1 - z) * 2 + core, e)
    blocks = ((1 - z) * 2, z * 2)
    core_copies = [[remote(core_out.at[k, i], core_in.at[k, i], 8 + 2 * k + i, other_core) for i in range(2)] for k in range(2)]
    pair_copies = [remote(pair_out.at[i], pair_in.at[i], 12 + i, other_pair) for i in range(2)]
    for i in range(2):
        values = rows[:, i].reshape(n_x * slots, width)
        total[i] = dot(wide[i * block : (i + 1) * block], values, NN).reshape(QUAD, share, width)
        core_out[0, i] = total[i, blocks[0] + 1 - core].astype(LOW)
        core_copies[0][i].start()
    for i in range(2):
        core_out[1, i] = total[i, blocks[1] + 1 - core].astype(LOW)
        core_copies[1][i].start()

    @pl.when(dp < n_tiles)
    def _():
        tiles_in[dp] = tiles[dp]
        all_of(tiles_in, n_dp - 1, 4, next_dp).wait_recv()
        sum_e[e] = jnp.sum(tiles_in[...], axis=0)

        @to_experts
        def _(peer):
            remote(sum_e.at[e], sum_e.at[e], 5, (dp, peer)).start()

    for i in range(2):
        core_copies[0][i].wait_recv()
        pair_out[i] = (total[i, blocks[0] + core] + core_in[0, i].astype(F32)).astype(LOW)
        pair_copies[i].start()

    @pl.when(dp < n_tiles)
    def _():
        all_of(sum_e, n_e - 1, 5, next_e).wait_recv()
        tiles_out[dp] = jnp.sum(sum_e[...], axis=0)

        @to_replicas
        def _(peer):
            remote(tiles_out.at[dp], tiles_out.at[dp], 6, (peer, e)).start()

    for i, out in enumerate((g1, g2)):
        core_copies[1][i].wait_recv()
        pair_copies[i].wait_recv()
        out[...] = (total[i, q] + core_in[1, i].astype(F32) + pair_in[i].astype(F32)).astype(LOW)

    @pl.when(dp < n_tiles)
    def _():
        all_of(tiles_out, n_tiles - 1, 6, next_dp).wait_recv()

    @pl.when(dp >= n_tiles)
    def _():
        all_of(tiles_out, n_tiles, 6, next_dp).wait_recv()

    for t in range(n_tiles):
        i, j = divmod(t, across)
        rg[i * tile_rows : (i + 1) * tile_rows, j * LANES : (j + 1) * LANES] = tiles_out[t]

    all_of(s1, n_e - 1, 0, next_e).wait_send()
    for s in range(1, half + 1):
        for copy in ring(s, 0):
            copy.wait_send()
    all_of(s2, n_e - 1, 2, next_e).wait_send()
    all_of(msgs, n_x - 1, 3, next_x).wait_send()
    for copy in core_copies[0] + core_copies[1] + pair_copies:
        copy.wait_send()

    @pl.when(dp < n_tiles)
    def _():
        all_of(tiles, n_tiles - 1, 4, next_dp).wait_send()
        all_of(sum_e, n_e - 1, 5, next_e).wait_send()
        all_of(tiles_in, n_dp - 1, 6, next_dp).wait_send()

    @pl.when(dp >= n_tiles)
    def _():
        all_of(tiles, n_tiles, 4, next_dp).wait_send()


def deliver(*refs):
    count = len(refs) // 2
    sems = refs[-1]
    copies = [pltpu.make_async_copy(refs[i], refs[count + i], sems.at[i]) for i in range(count)]
    for copy in copies:
        copy.start()
    for copy in copies:
        copy.wait()


def on_device(n_dp, n_e, tokens, cotangent, router, in_weights, out_weights):
    _, patches, width = tokens.shape
    ff = in_weights.shape[2]
    slots = router.shape[1]
    n_x = n_dp // QUAD
    share = ff // n_dp
    tile_rows = min(8, slots)
    n_tiles = slots // tile_rows * (width // LANES)
    vmem = pltpu.VMEM
    dma = pltpu.SemaphoreType.DMA
    shapes = (
        ((patches, width), LOW),
        ((slots, width), F32),
        ((share, width), LOW),
        ((share, width), LOW),
    )
    results = pl.pallas_call(
        functools.partial(kernel, n_dp, n_e),
        out_shape=[vmem(*shape) for shape in shapes],
        in_specs=[pl.BlockSpec(memory_space=pl.ANY)] * 5,
        out_specs=[pl.BlockSpec(memory_space=vmem)] * 4,
        scratch_shapes=[
            vmem((patches, width), LOW),
            vmem((patches, width), LOW),
            vmem((slots, width), LOW),
            vmem((width, ff), LOW),
            vmem((ff, width), LOW),
            vmem((slots * ROWS, LANES), F32),
            vmem((slots * ROWS, LANES), F32),
            *[vmem((slots, ROWS, LANES), LOW)] * 4,
            vmem((n_x, 2, slots, width), LOW),
            vmem((n_x, slots, 2 * ff // n_x), LOW),
            vmem((n_x, slots, 2 * ff // n_x), LOW),
            vmem((2, QUAD, share, width), F32),
            vmem((n_tiles, tile_rows, LANES), F32),
            vmem((n_dp, tile_rows, LANES), F32),
            vmem((n_e, tile_rows, LANES), F32),
            vmem((n_tiles, tile_rows, LANES), F32),
            vmem((2, 2, share, width), LOW),
            vmem((2, 2, share, width), LOW),
            vmem((2, share, width), LOW),
            vmem((2, share, width), LOW),
            dma((5,)),
            dma((14,)),
            dma((14,)),
            dma((n_x // 2, 2)),
            dma((n_x // 2, 2)),
        ],
        compiler_params=pltpu.CompilerParams(
            collective_id=0, has_side_effects=True, vmem_limit_bytes=56 * 2**20
        ),
        cost_estimate=pl.CostEstimate(flops=10**9, bytes_accessed=10**7, transcendentals=10**5),
    )(tokens[0], cotangent[0], router.T, in_weights[0], out_weights[0])
    token_grad, router_grad, in_grad, out_grad = pl.pallas_call(
        deliver,
        out_shape=[jax.ShapeDtypeStruct(*shape) for shape in shapes],
        in_specs=[pl.BlockSpec(memory_space=vmem)] * 4,
        out_specs=[pl.BlockSpec(memory_space=pl.ANY)] * 4,
        scratch_shapes=[dma((4,))],
    )(*[pltpu.with_memory_space_constraint(result, vmem) for result in results])
    return token_grad[None], router_grad.T, in_grad[:, None], out_grad[:, None]


def solution(mesh):
    image = P(("dp", "expert"), None, None)
    expert = P("expert", None, None)
    grad = P("dp", "expert", None)
    return jax.shard_map(
        functools.partial(on_device, mesh.shape["dp"], mesh.shape["expert"]),
        mesh=mesh,
        in_specs=(image, image, P(), expert, expert),
        out_specs=(image, P(), grad, grad),
        check_vma=False,
    )
```

time: 79.1 us -> 72.5 us (0.917)
  local copies, waits for them, and re-layouts: 4.97 us -> 0 us
  Pallas kernels: 73.3 us -> 71.7 us
    unnamed x2 -> x0, local copies, waits for them, and re-layouts: 3.3 us -> none
    another operation x1 -> x0, local copies, waits for them, and re-layouts: 1.67 us -> none  [on_device(): weight_grads[1][:, None]]
    pallas_call x1 -> x2, Pallas kernels: 73.3 us -> 71.7 us  [the longest x1 70.8 us: on_device(): pl.pallas_call(functools.partial(kernel, n_dp, n_e), out_shape=[vmem(*sha...]
where the time goes in v2:
time: 72.5 us; the launch traced here: 72.4 us
  Pallas kernels  71.7 us (99%)
    pallas_call x1, Pallas kernels, on_device(): pl.pallas_call(functools.partial(kernel, n_dp, n_e), out_shape=[vmem(*sha...  70.8 us

profile of v2, /device:TPU:1, one launch (start us, length us, event | category | flops | bytes accessed | tf_op | source)
XLA Modules:
  0.0 72.4 jit_solution(3851987337931516034)
XLA Ops:
  0.6 70.8 %shard_map.84 = (bf16[256,768]{1,0:T(8,128)(2,1)S(1)}, f32[32,768]{1,0:T(8,128)S(1)}, bf16[80,768]{1,0:T(8,128)(2,1)S(1)}, bf16[80,768]{1,0:T(8,128)(2,1)S(1)}) custom-call(bf16[256,768]{1,0:T(8,128)(2,1)} %bitcast.11, bf16[256,768]{1,0:T(8,128)(2,1)} %bitcast.12, bf16[32,768]{1,0:T(8,128)(2,1)} %bitcast.13, bf16[768,2560]{1,0:T(8,128)(2,1)} %bitcast.9, ...), custom_call_target="tpu_custom_call" | custom-call | flops 1000000000 | bytes 10000000 | tf_op jit(solution)/shard_map/pallas_call | solution.py:332
  71.5 0.9 %shard_map.85 = (bf16[256,768]{1,0:T(8,128)(2,1)}, f32[32,768]{1,0:T(8,128)}, bf16[80,768]{1,0:T(8,128)(2,1)}, bf16[80,768]{1,0:T(8,128)(2,1)}) custom-call(bf16[256,768]{1,0:T(8,128)(2,1)S(1)} %get-tuple-element.12.refs_0_, f32[32,768]{1,0:T(8,128)S(1)} %get-tuple-element.13.refs_1_, bf16[80,768]{1,0:T(8,128)(2,1)S(1)} %get-tuple-element.14.refs_2_, ...), custom_call_target="tpu_custom_call" | custom-call | tf_op jit(solution)/shard_map/pallas_call | solution.py:369

commit v3 on v2

--- a/solution.py
+++ b/solution.py
@@ -67,6 +67,25 @@
     tile_rows = tiles.shape[1]
     across = width // LANES
 
+    def each(count, body):
+        far = max(1, count * 3 // 8)
+        for o in (*range(far, count), *range(1, far)):
+            body(o)
+
+    def to_experts(body):
+        each(n_e, lambda o: body(lax.rem(e + o, n_e)))
+
+    def to_replicas(body):
+        each(n_dp, lambda o: body(lax.rem(dp + o, n_dp)))
+
+    barrier = pltpu.get_barrier_semaphore()
+
+    def greet(device):
+        pl.semaphore_signal(barrier, inc=1, device_id=device, device_id_type=MESH)
+
+    to_experts(lambda peer: greet((dp, peer)))
+    to_replicas(lambda peer: greet((peer, e)))
+
     loads = [
         pltpu.make_async_copy(src, dst, load.at[i])
         for i, (src, dst) in enumerate(((rt_h, rt), (tok_h, tok), (cot_h, cot), (w1_h, w1), (w2_h, w2)))
@@ -74,25 +93,6 @@
     for copy in loads:
         copy.start()
     stage[...] = jnp.zeros_like(stage)
-
-    def each(count, body):
-        far = max(1, count * 3 // 8)
-        for o in (*range(far, count), *range(1, far)):
-            body(o)
-
-    def to_experts(body):
-        each(n_e, lambda o: body(lax.rem(e + o, n_e)))
-
-    def to_replicas(body):
-        each(n_dp, lambda o: body(lax.rem(dp + o, n_dp)))
-
-    barrier = pltpu.get_barrier_semaphore()
-
-    def greet(device):
-        pl.semaphore_signal(barrier, inc=1, device_id=device, device_id_type=MESH)
-
-    to_experts(lambda peer: greet((dp, peer)))
-    to_replicas(lambda peer: greet((peer, e)))
 
     def remote(src, dst, at, device):
         return pltpu.make_async_remote_copy(
@@ -185,20 +185,20 @@
             at = 2 * (k * per + i)
             msgs[at] = jnp.where(is_first, p_part, pltpu.roll(h_part, block, 1)).astype(LOW)
             msgs[at + 1] = jnp.where(is_first, pltpu.roll(p_part, block, 1), h_part).astype(LOW)
+            for to in (at, at + 1):
+
+                @pl.when(x != to)
+                def _():
+                    remote(msgs.at[to], part.at[x], 3, (to * QUAD + q, e)).start()
     pack(stage, s2, outputs, grads)
 
     @to_experts
     def _(peer):
         remote(s2.at[peer], r2.at[e], 2, (dp, peer)).start()
 
-    @functools.partial(each, n_x)
-    def _(o):
-        peer = lax.rem(x + o, n_x)
-        remote(msgs.at[peer], part.at[x], 3, (peer * QUAD + q, e)).start()
-
     part[x] = msgs[x]
     r2[e] = s2[e]
-    for s in range(1, half):
+    for s in range(1, half - 1):
         ring_arrived(s)
         ring_start(s + 1)
     all_of(r2, n_e - 1, 2, next_e).wait_recv()
@@ -220,9 +220,22 @@
         def _():
             remote(tiles.at[peer], tiles_in.at[dp], 4, (peer, e)).start()
 
+    if half > 1:
+        ring_arrived(half - 1)
+        ring_start(half)
     weights = jnp.concatenate([dispatch_low, logit_low], axis=0)
     values = jnp.concatenate([input_grads, rt[...]], axis=0)
     tg[...] = dot(weights, values, TN).astype(LOW)
+
+    @pl.when(dp < n_tiles)
+    def _():
+        tiles_in[dp] = tiles[dp]
+        all_of(tiles_in, n_dp - 1, 4, next_dp).wait_recv()
+        sum_e[e] = jnp.sum(tiles_in[...], axis=0)
+
+        @to_experts
+        def _(peer):
+            remote(sum_e.at[e], sum_e.at[e], 5, (dp, peer)).start()
 
     ring_arrived(half)
     all_of(part, n_x - 1, 3, next_x).wait_recv()
@@ -241,16 +254,6 @@
     for i in range(2):
         core_out[1, i] = total[i, blocks[1] + 1 - core].astype(LOW)
         core_copies[1][i].start()
-
-    @pl.when(dp < n_tiles)
-    def _():
-        tiles_in[dp] = tiles[dp]
-        all_of(tiles_in, n_dp - 1, 4, next_dp).wait_recv()
-        sum_e[e] = jnp.sum(tiles_in[...], axis=0)
-
-        @to_experts
-        def _(peer):
-            remote(sum_e.at[e], sum_e.at[e], 5, (dp, peer)).start()
 
     for i in range(2):
         core_copies[0][i].wait_recv()

time: 72.5 us -> 67.6 us (0.932)
  Pallas kernels: 71.7 us -> 66.8 us
    pallas_call x1, Pallas kernels: 70.8 us -> 65.9 us  [on_device(): pl.pallas_call(functools.partial(kernel, n_dp, n_e), out_shape=[vmem(*sha...]
where the time goes in v3:
time: 67.6 us; the launch traced here: 67.4 us
  Pallas kernels  66.8 us (99%)
    pallas_call x1, Pallas kernels, on_device(): pl.pallas_call(functools.partial(kernel, n_dp, n_e), out_shape=[vmem(*sha...  65.9 us

profile of v3, /device:TPU:1, one launch (start us, length us, event | category | flops | bytes accessed | tf_op | source)
XLA Modules:
  0.0 67.4 jit_solution(8355097468859433449)
XLA Ops:
  0.6 65.9 %shard_map.84 = (bf16[256,768]{1,0:T(8,128)(2,1)S(1)}, f32[32,768]{1,0:T(8,128)S(1)}, bf16[80,768]{1,0:T(8,128)(2,1)S(1)}, bf16[80,768]{1,0:T(8,128)(2,1)S(1)}) custom-call(bf16[256,768]{1,0:T(8,128)(2,1)} %bitcast.11, bf16[256,768]{1,0:T(8,128)(2,1)} %bitcast.12, bf16[32,768]{1,0:T(8,128)(2,1)} %bitcast.13, bf16[768,2560]{1,0:T(8,128)(2,1)} %bitcast.9, ...), custom_call_target="tpu_custom_call" | custom-call | flops 1000000000 | bytes 10000000 | tf_op jit(solution)/shard_map/pallas_call | solution.py:335
  66.5 0.9 %shard_map.85 = (bf16[256,768]{1,0:T(8,128)(2,1)}, f32[32,768]{1,0:T(8,128)}, bf16[80,768]{1,0:T(8,128)(2,1)}, bf16[80,768]{1,0:T(8,128)(2,1)}) custom-call(bf16[256,768]{1,0:T(8,128)(2,1)S(1)} %get-tuple-element.12.refs_0_, f32[32,768]{1,0:T(8,128)S(1)} %get-tuple-element.13.refs_1_, bf16[80,768]{1,0:T(8,128)(2,1)S(1)} %get-tuple-element.14.refs_2_, ...), custom_call_target="tpu_custom_call" | custom-call | tf_op jit(solution)/shard_map/pallas_call | solution.py:372

commit v4 on v3

--- a/solution.py
+++ b/solution.py
@@ -198,7 +198,7 @@
 
     part[x] = msgs[x]
     r2[e] = s2[e]
-    for s in range(1, half - 1):
+    for s in range(1, half - 2):
         ring_arrived(s)
         ring_start(s + 1)
     all_of(r2, n_e - 1, 2, next_e).wait_recv()
@@ -220,12 +220,16 @@
         def _():
             remote(tiles.at[peer], tiles_in.at[dp], 4, (peer, e)).start()
 
+    for s in range(max(1, half - 2), half - 1):
+        ring_arrived(s)
+        ring_start(s + 1)
+    weights = jnp.concatenate([dispatch_low, logit_low], axis=0)
+    values = jnp.concatenate([input_grads, rt[...]], axis=0)
+    tg[...] = dot(weights, values, TN).astype(LOW)
+
     if half > 1:
         ring_arrived(half - 1)
         ring_start(half)
-    weights = jnp.concatenate([dispatch_low, logit_low], axis=0)
-    values = jnp.concatenate([input_grads, rt[...]], axis=0)
-    tg[...] = dot(weights, values, TN).astype(LOW)
 
     @pl.when(dp < n_tiles)
     def _():

time: 67.6 us -> 66.1 us (0.978)
  Pallas kernels: 66.8 us -> 65.3 us
    pallas_call x1, Pallas kernels: 65.9 us -> 64.4 us  [on_device(): pl.pallas_call(functools.partial(kernel, n_dp, n_e), out_shape=[vmem(*sha...]
where the time goes in v4:
time: 66.1 us; the launch traced here: 66 us
  Pallas kernels  65.3 us (99%)
    pallas_call x1, Pallas kernels, on_device(): pl.pallas_call(functools.partial(kernel, n_dp, n_e), out_shape=[vmem(*sha...  64.4 us

profile of v4, /device:TPU:1, one launch (start us, length us, event | category | flops | bytes accessed | tf_op | source)
XLA Modules:
  0.0 66.0 jit_solution(11227082689484477284)
XLA Ops:
  0.6 64.4 %shard_map.84 = (bf16[256,768]{1,0:T(8,128)(2,1)S(1)}, f32[32,768]{1,0:T(8,128)S(1)}, bf16[80,768]{1,0:T(8,128)(2,1)S(1)}, bf16[80,768]{1,0:T(8,128)(2,1)S(1)}) custom-call(bf16[256,768]{1,0:T(8,128)(2,1)} %bitcast.11, bf16[256,768]{1,0:T(8,128)(2,1)} %bitcast.12, bf16[32,768]{1,0:T(8,128)(2,1)} %bitcast.13, bf16[768,2560]{1,0:T(8,128)(2,1)} %bitcast.9, ...), custom_call_target="tpu_custom_call" | custom-call | flops 1000000000 | bytes 10000000 | tf_op jit(solution)/shard_map/pallas_call | solution.py:339
  65.1 0.9 %shard_map.85 = (bf16[256,768]{1,0:T(8,128)(2,1)}, f32[32,768]{1,0:T(8,128)}, bf16[80,768]{1,0:T(8,128)(2,1)}, bf16[80,768]{1,0:T(8,128)(2,1)}) custom-call(bf16[256,768]{1,0:T(8,128)(2,1)S(1)} %get-tuple-element.12.refs_0_, f32[32,768]{1,0:T(8,128)S(1)} %get-tuple-element.13.refs_1_, bf16[80,768]{1,0:T(8,128)(2,1)S(1)} %get-tuple-element.14.refs_2_, ...), custom_call_target="tpu_custom_call" | custom-call | tf_op jit(solution)/shard_map/pallas_call | solution.py:376
